TPU v7x, 512 devices: a whole 4x8x8 slice. The times are simulated.
512 devices in a mesh: box: 512 (over x, z, y, core).
Axes of the slice: x: 4, y: 8, z: 8, core: 2. Of those that a mesh axis runs over, the one named last changes fastest.
Arguments:
- coords: float32 [3, 1048576], P(None, 'box'), may hold values from 0 to 1
- loads: bfloat16 [8, 1048576], P(None, 'box'), may hold values from -6 to 6
- occupancy: int32 [4096], P('box'), may hold values from 64 to 256, as said below
- basis: bfloat16 [4096, 64, 256], P('box'), may hold values from -0.375 to 0.375
- transfer: float32 [6, 2, 64, 64], replicated, may hold values from -0.5 to 0.5
Outputs:
- potential: float32 [8, 1048576], P(None, 'box')
Inputs may be any that keep to these rules, and one draw needn't show every extreme that they name: occupancy[l] is the number of live centres of leaf l; they fill its first slots, and every leaf keeps at least its 64 skeleton centres.
All inputs are finite; a program needn't handle non-finite values.
Results may differ from a plain program's by a relative error of at most 0.0029.
Values sent between devices are 32-bit elements; how exact they have to be, the bound alone decides.
A program may use at most 64 MiB of HBM per device.

v0:
```python
import functools

import jax
import jax.numpy as jnp
from jax import lax
from jax.experimental import pallas as pl
from jax.experimental.pallas import tpu as pltpu
from jax.sharding import PartitionSpec as P

LEAF = 256
COLS = 8
LEAVES = 8
MEMBERS = 8
OWN = LEAF * LEAVES

f32 = jnp.float32
bf16 = jnp.bfloat16
soften = 0.0001
near_scale = 0.0625
far_scale = 0.125
NN = (((1,), (0,)), ((), ()))
NT = (((1,), (1,)), ((), ()))
MESH = pl.DeviceIdType.MESH


def div(a, b):
    return lax.div(a, jnp.int32(b))


def rem(a, b):
    return lax.rem(a, jnp.int32(b))


def phi(tx, ty, tz, sx, sy, sz, scale):
    dx = tx - sx
    dy = ty - sy
    dz = tz - sz
    r2 = dx * dx + dy * dy + dz * dz
    return (r2 * (0.5 * scale)) * jnp.log(r2 + soften)


def split(x):
    high = x.astype(bf16)
    return high, (x - high.astype(f32)).astype(bf16)


def mm(a, b, dims):
    rows = a.shape[0]
    high = a.astype(bf16).astype(f32)
    stacked = jnp.concatenate([high, a - high], axis=0).astype(bf16)
    both = lax.dot_general(stacked, b[0][...], dims, preferred_element_type=f32)
    low = lax.dot_general(stacked[:rows], b[1][...], dims, preferred_element_type=f32)
    return both[:rows] + (both[rows:] + low)


def low_half(shape):
    return lax.broadcasted_iota(jnp.int32, shape, len(shape) - 1) < 64


def merge(rows):
    count = rows.shape[0] // 16
    low = low_half((8, 128))
    return [
        jnp.where(low, rows[16 * i : 16 * i + 8], rows[16 * i + 8 : 16 * i + 16])
        for i in range(count)
    ]


def raise_coef(pairs, level_map):
    rows = mm(jnp.concatenate(pairs, axis=0), level_map, NN)
    return merge(rows) if len(pairs) > 1 else [rows]


def pick(x, entries):
    rows = x.shape[0]
    a = x.astype(bf16).astype(f32)
    b = (x - a).astype(bf16).astype(f32)
    c = (x - a) - b
    stacked = jnp.concatenate([a, b, c], axis=0).astype(bf16)
    picked = lax.dot_general(stacked, entries, NN, preferred_element_type=f32)
    return picked[:rows] + picked[rows : 2 * rows] + picked[2 * rows :]


def raise_skel(pairs, every_second):
    rows_up = pick(jnp.concatenate(pairs, axis=0), every_second)
    return merge(rows_up) if len(pairs) > 1 else [rows_up]


def cousins(chain, slot):
    low = low_half((8, 128))
    column = chain[slot, 1].T
    tx, ty, tz = column[:, 0:1], column[:, 1:2], column[:, 2:3]
    before, after = chain[slot - 1, 0], chain[slot + 1, 0]
    tiles = []
    for skel in (chain[slot - 1, 1], chain[slot + 1, 1]):
        tiles.append(phi(tx, ty, tz, skel[0:1], skel[1:2], skel[2:3], far_scale))
    tile = jnp.concatenate(tiles, axis=1)
    even = jnp.concatenate([jnp.where(low, before, 0.0), after], axis=1)
    odd = jnp.concatenate([before, jnp.where(low, 0.0, after)], axis=1)
    rows = mm(jnp.concatenate([even, odd], axis=0), split(tile), NT)
    return jnp.where(low, rows[:8], rows[8:])


def lower(pairs, level_map):
    height = pairs[0].shape[0]
    low = low_half((height, 128))
    stacked = []
    for pair in pairs:
        stacked += [jnp.where(low, pair, 0.0), jnp.where(low, 0.0, pair)]
    rows = mm(jnp.concatenate(stacked, axis=0), level_map, NT)
    return [rows[height * i : height * (i + 1)] for i in range(2 * len(pairs))]


def kernel(
    boxes,
    across,
    coords_hbm,
    loads_hbm,
    occ_hbm,
    basis_hbm,
    transfer_hbm,
    out_ref,
    coords,
    loads,
    occ,
    basis,
    transfer,
    map_high,
    map_low,
    path_map,
    field,
    column,
    leaf_high,
    leaf_low,
    near,
    tile_a,
    tile_b,
    tile_c,
    chain,
    g_chain,
    local,
    edge_send,
    edge_recv,
    u_buf,
    g_buf,
    bound_send,
    bound_recv,
    quad_recv,
    rim_recv,
    far_send,
    far_buf,
    part_buf,
    load_sem,
    near_send_sem,
    near_recv_sem,
    edge_send_sem,
    edge_recv_sem,
    u_send_sem,
    u_recv_sem,
    g_send_sem,
    g_recv_sem,
    bound_send_sem,
    bound_recv_sem,
    rim_send_sem,
    rim_recv_sem,
    far_send_sem,
    far_recv_sem,
    part_send_sem,
    part_recv_sem,
    ready,
):
    loading = [
        pltpu.make_async_copy(src, dst, load_sem.at[at])
        for at, (src, dst) in enumerate(
            [
                (coords_hbm, coords),
                (transfer_hbm, transfer),
                (loads_hbm, loads),
                (occ_hbm, occ),
                (basis_hbm, basis),
            ]
        )
    ]
    for copy in loading:
        copy.start()

    device = lax.axis_index("box")
    total = boxes * MEMBERS
    strides = boxes // MEMBERS
    depth = boxes // (2 * across)
    box, member = div(device, MEMBERS), rem(device, MEMBERS)
    x, z, y_half = div(box, 2 * depth), rem(div(box, 2), depth), rem(box, 2)
    y, core = div(member, 2), rem(member, 2)
    low = low_half((8, 128))
    half = jnp.where(low, 0, 1)

    top = jnp.where(y == 3, 1, 0)
    outer = jnp.where(y == 0, 1, top)
    side_to = jnp.where(outer == 1, top, 2 - y)
    side_from = jnp.where(outer == 1, 1 - top, 2 - y)
    far_half = jnp.where(outer == 1, 1 - y_half, y_half)
    z_core = rem(div(z, 2), 2)
    far_member = 2 * jnp.where(outer == 1, 3 - y, y) + z_core
    z_high, z_low = div(z, 4), rem(z, 2)
    far_x = [rem(x + dx, across) for dx in range(across)]
    far_steps = [(dx, turn) for dx in range(across) for turn in range(2)]

    def far_depths(side):
        first = 4 * rem(side + z_high, 2) + 2 * core
        return [first + z_low, first + 1 - z_low]

    to_z, from_z = far_depths(side_to), far_depths(side_from)

    def far_box(depths, dx, turn):
        return (far_x[dx % across] * depth + depths[turn]) * 2 + far_half

    far_to = [far_box(to_z, dx, turn) * MEMBERS + far_member for dx, turn in far_steps]
    far_from = [far_box(from_z, -dx, turn) for dx, turn in far_steps]
    alone = jnp.logical_and(jnp.logical_and(outer == 0, side_to == 0), core == z_core)

    barrier = pltpu.get_barrier_semaphore()

    def greet(target):
        pl.semaphore_signal(barrier, inc=1, device_id=(target,), device_id_type=MESH)

    def order(at):
        return jnp.where(at == 0, 0, jnp.where(at >= 6, 2, 1))

    mine = order(z)
    to_later = [jnp.where(order(at) > mine, 1, 0) for at in to_z]
    from_earlier = [jnp.where(order(at) < mine, 1, 0) for at in from_z]
    far_order = [(2 * dx + turn) for turn in range(2) for dx in (2, 1, 3, 0)]

    def far_each(turn, act):
        for k in far_order[4 * turn : 4 * turn + 4]:
            if k:
                act(k)
            else:
                pl.when(jnp.logical_not(alone))(functools.partial(act, 0))

    for turn in range(2):

        @pl.when(from_earlier[turn] == 0)
        def _(turn=turn):
            far_each(turn, lambda k: greet(far_from[k] * MEMBERS + far_member))

        @pl.when(to_later[turn] == 1)
        def _(turn=turn):
            far_each(turn, lambda k: greet(far_to[k]))

    left_device = rem(device + total - 1, total)
    right_device = rem(device + 1, total)
    mirror = 2 * (3 - y) + core
    left_box = rem(box + boxes - 1, boxes) * MEMBERS + mirror
    right_box = rem(box + 1, boxes) * MEMBERS + mirror
    mates = [box * MEMBERS + rem(member + r, MEMBERS) for r in (6, 2, 7, 3, 5, 4, 1)]
    at_rim = outer == 1
    rim_box = rem(box + boxes + 2 * top - 1, boxes)
    rim_devices = [rim_box * MEMBERS + 6 - 6 * top + t for t in range(2)]
    quad = div(member, 4)
    quad_device = rem(box + boxes + 2 * quad - 1, boxes) * MEMBERS + mirror
    early = jnp.where(z == 0, 1, 0)
    ahead = 2
    before = [device > 0, box > 0]
    after = [device < total - 1, box < boxes - 1]
    inside = jnp.where(quad == 0, box, boxes - 1 - box) > 0
    open_rim = jnp.logical_and(at_rim, inside)

    for target in mates:
        greet(target)
    for has, targets in ((before, (left_device, left_box)), (after, (right_device, right_box))):
        for at in range(2):
            pl.when(has[at])(functools.partial(greet, targets[at]))

    @pl.when(open_rim)
    def _():
        for target in rim_devices:
            greet(target)

    lanes = lax.broadcasted_iota(jnp.int32, (1, 128), 1)
    index = lax.broadcasted_iota(jnp.int32, (512, 128), 0)
    placed = (index == (lanes - 64 - 8 * member) * 64).astype(f32).astype(bf16)
    picks = (lax.broadcasted_iota(jnp.int32, (1, 128), 1) & 63) * 2
    every_second = (
        (lax.broadcasted_iota(jnp.int32, (128, 128), 0) == picks).astype(f32).astype(bf16)
    )
    for copy in loading:
        copy.wait()
    points = jnp.concatenate([coords[...], jnp.zeros((5, OWN), f32)], axis=0)
    s0 = [
        jnp.concatenate(
            [points[:, 512 * p : 512 * p + 64], points[:, 512 * p + 256 : 512 * p + 320]], axis=1
        )
        for p in range(4)
    ]
    s6 = pick(jnp.concatenate(s0, axis=1), placed)

    maps = [(map_high.at[level], map_low.at[level]) for level in range(6)]

    def set_map(level):
        once = transfer[level]
        map_high[level], map_low[level] = split(jnp.concatenate([once, once], axis=1))

    for level in range(2):
        set_map(level)
    slots = lax.broadcasted_iota(jnp.int32, (COLS, LEAF), 1)
    live = []
    for leaf in range(LEAVES):
        part = loads[:, leaf * LEAF : (leaf + 1) * LEAF].astype(f32)
        live.append(jnp.where(slots < occ[leaf], part, 0.0))
    c0 = []
    for p in range(4):
        two = jnp.concatenate([live[2 * p], live[2 * p + 1]], axis=0).astype(bf16)
        rows = lax.dot_general(
            two, basis[128 * p : 128 * p + 128, :], NT, preferred_element_type=f32
        )
        c0.append(jnp.where(low, rows[:8], rows[8:]))
    c1 = raise_coef(c0, maps[0])
    c2 = raise_coef(c1, maps[1])
    def factor(level, at):
        return transfer[level, pl.ds(pl.multiple_of(64 * at, 64), 64), :]

    map_34 = mm(transfer[2], split(factor(3, core)), NN)
    wide = jnp.concatenate([factor(5, quad), jnp.zeros((64, 64), f32)], axis=1)
    map_56 = mm(factor(4, rem(y, 2)), split(wide), NN)
    map_6 = mm(map_34, split(map_56), NN)
    u_buf[member] = mm(c2[0], split(map_6), NN) + s6
    path_map[...] = map_6

    def set_field():
        field[0, :, LEAF : LEAF + OWN] = points
        for leaf in range(LEAVES):
            field[1, :, (leaf + 1) * LEAF : (leaf + 2) * LEAF] = live[leaf]
        for at in range(0, OWN, 128):
            column[at : at + 128, :] = points[:, at : at + 128].T
        near[...] = jnp.zeros_like(near)

    def fill_tile(tile, row, col, width):
        sx = field[0, 0:1, pl.ds(col, width)]
        sy = field[0, 1:2, pl.ds(col, width)]
        sz = field[0, 2:3, pl.ds(col, width)]
        for at in range(0, LEAF, 16):
            rows = column[pl.ds(row + at, 16), :]
            tile[at : at + 16, 0:width] = phi(
                rows[:, 0:1], rows[:, 1:2], rows[:, 2:3], sx, sy, sz, near_scale
            ).astype(bf16)

    def near_leaf(tile, row):
        col = row + LEAF
        fill_tile(tile, row, col, 2 * LEAF)
        loads_two = field[1, :, pl.ds(col, 2 * LEAF)].astype(bf16)
        this = lax.dot_general(loads_two, tile[...], NT, preferred_element_type=f32)
        after = lax.dot_general(
            loads_two[:, :LEAF], tile[:, LEAF:], NN, preferred_element_type=f32
        )
        return this, after

    def near_two(row):
        first, second_part = near_leaf(tile_a, row)
        second, third = near_leaf(tile_b, row + LEAF)
        near[:, pl.ds(row, LEAF)] += first
        near[:, pl.ds(row + LEAF, LEAF)] += second_part + second
        near[:, pl.ds(row + 2 * LEAF, LEAF)] += third

    def near_step(pair, carry):
        near_two(pl.multiple_of(pair * (2 * LEAF), 2 * LEAF))
        return carry

    def side(block, at):
        lanes = jnp.where(low_half((1, 128)), 0, 1)
        return jnp.where(lanes == at, block, 0.0)

    def set_chain(levels, into):
        for at, (pairs, skels) in enumerate(levels):
            first = (1, 7, 11)[at]
            for p in range(len(pairs)):
                into[first + p, 0] = pairs[p]
                into[first + p, 1] = skels[p]

    def set_inner():
        row = (LEAVES - 2) * LEAF
        this, after = near_leaf(tile_a, row)
        fill_tile(tile_c, row + LEAF, row + 2 * LEAF, LEAF)
        own = field[1, :, row + 2 * LEAF : row + 3 * LEAF].astype(bf16)
        after += lax.dot_general(own, tile_c[...], NT, preferred_element_type=f32)
        near[:, row : row + LEAF] += this
        near[:, row + LEAF : row + 2 * LEAF] += after
        for slot in (2, 3):
            local[slot - 1] = cousins(chain, slot)

    def set_edges():
        s1 = raise_skel(s0, every_second)
        s2 = raise_skel(s1, every_second)

        set_chain([(c0, s0), (c1, s1), (c2, s2)], chain)
        for at, (pairs, skels) in enumerate([(c0, s0), (c1, s1), (c2, s2)]):
            edge_send[0, at, 0] = pairs[-1]
            edge_send[0, at, 1] = skels[-1]
            edge_send[1, at, 0] = pairs[0]
            edge_send[1, at, 1] = skels[0]
    def set_leaf_paths():
        x2 = jnp.concatenate([path_map[...].T[:64], transfer[2].T], axis=0)
        x0 = lower(lower([x2], maps[1]), maps[0])
        leaf_high[...], leaf_low[...] = split(jnp.concatenate(x0, axis=1))

    @pl.when(early == 1)
    def _():
        set_field()
        lax.fori_loop(0, ahead, near_step, 0)

    pl.semaphore_wait(
        barrier,
        MEMBERS - 1
        + sum(has.astype(jnp.int32) for has in before + after)
        + 2 * open_rim.astype(jnp.int32)
        + 4 * (2 - to_later[0] - to_later[1])
        - alone.astype(jnp.int32)
        + 4 * (from_earlier[0] + from_earlier[1]),
    )

    def tell(target):
        pl.semaphore_signal(ready, inc=1, device_id=(target,), device_id_type=MESH)

    for turn in range(2):

        @pl.when(from_earlier[turn] == 1)
        def _(turn=turn):
            far_each(turn, lambda k: tell(far_from[k] * MEMBERS + far_member))

    def remote(src, dst, send_sem, recv_sem, target):
        return pltpu.make_async_remote_copy(
            src_ref=src,
            dst_ref=dst,
            send_sem=send_sem,
            recv_sem=recv_sem,
            device_id=(target,),
            device_id_type=MESH,
        )

    def send(*ends):
        copy = remote(*ends)
        copy.start()
        return copy

    def wait_all(ref, semaphore):
        pltpu.make_async_copy(ref, ref, semaphore).wait()

    for mate in mates:
        send(u_buf.at[member], u_buf.at[member], u_send_sem, u_recv_sem, mate)

    set_map(2)
    every_eighth = (index == (lanes & 63) * 8).astype(f32).astype(bf16)
    s3 = pick(jnp.concatenate(s0, axis=1), every_eighth)
    c3 = raise_coef(c2, maps[2])[0]
    g_buf[member] = jnp.where(half == core, c3, s3)
    for mate in mates:
        send(g_buf.at[member], g_buf.at[member], g_send_sem, g_recv_sem, mate)

    rim_copies = [
        pltpu.make_async_remote_copy(
            src_ref=g_buf.at[member],
            dst_ref=rim_recv.at[core],
            send_sem=rim_send_sem.at[t],
            recv_sem=rim_recv_sem.at[core],
            device_id=(rim_devices[t],),
            device_id_type=MESH,
        )
        for t in range(2)
    ]

    @pl.when(open_rim)
    def _():
        for copy in rim_copies:
            copy.start()

    @pl.when(early == 0)
    def _():
        set_field()

    last = LEAF * LEAVES
    near_copies = [
        remote(
            field.at[:, :, last : last + LEAF],
            field.at[:, :, 0:LEAF],
            near_send_sem.at[0],
            near_recv_sem.at[0],
            right_device,
        ),
        remote(
            field.at[:, :, LEAF : 2 * LEAF],
            field.at[:, :, last + LEAF : last + 2 * LEAF],
            near_send_sem.at[1],
            near_recv_sem.at[1],
            left_device,
        ),
    ]

    def start(copies, at=0):
        for copy, has in zip(copies, (after[at], before[at])):
            pl.when(has)(copy.start)

    def receive(copies, at=0):
        for copy, has in zip(copies, (before[at], after[at])):
            pl.when(has)(copy.wait_recv)

    start(near_copies)

    edge_copies = [
        remote(
            edge_send.at[side],
            edge_recv.at[side],
            edge_send_sem.at[side],
            edge_recv_sem.at[side],
            (right_device, left_device)[side],
        )
        for side in range(2)
    ]

    set_edges()
    start(edge_copies)

    set_map(3)
    set_map(4)

    @pl.when(early == 1)
    def _():
        set_leaf_paths()

    wait_all(u_buf.at[pl.ds(0, MEMBERS - 1)], u_recv_sem)
    parts = [u_buf[at] for at in range(MEMBERS)]
    while len(parts) > 1:
        parts = [a + b for a, b in zip(parts[0::2], parts[1::2])]
    top_record = parts[0]
    swapped_record = pltpu.roll(top_record, 64, 1)
    far_send[0] = top_record
    far_send[1] = swapped_record

    @pl.when(alone)
    def _():
        far_buf[0] = far_send[0]

    def far_copy(k):
        return remote(
            far_send.at[k % 2],
            far_buf.at[k],
            far_send_sem.at[min(k, 1)],
            far_recv_sem.at[min(k, 1)],
            far_to[k],
        )

    first_far = far_copy(0)
    for turn in range(2):

        @pl.when(to_later[turn] == 0)
        def _(turn=turn):
            far_each(turn, lambda k: far_copy(k).start())

    wait_all(g_buf.at[pl.ds(0, MEMBERS - 1)], g_recv_sem)
    c3s, s3s = [], []
    for p in range(4):
        even, odd = g_buf[2 * p], g_buf[2 * p + 1]
        c3s.append(jnp.where(low, even, odd))
        s3s.append(pltpu.roll(jnp.where(low, odd, even), 64, 1))
    c4s, s4s = raise_coef(c3s, maps[3]), raise_skel(s3s, every_second)
    c5s, s5s = raise_coef(c4s, maps[4]), raise_skel(s4s, every_second)
    set_chain([(c3s, s3s), (c4s, s4s), (c5s, s5s)], g_chain)
    for at in range(2):
        bound_send[at, 0] = c5s[0]
        bound_send[at, 1] = s5s[0] + pltpu.roll(s4s[1 - at], 3, 0)
    bound_copies = [
        remote(
            bound_send.at[side],
            bound_recv.at[side],
            bound_send_sem.at[side],
            bound_recv_sem.at[side],
            (right_box, left_box)[side],
        )
        for side in range(2)
    ]
    quad_copy = remote(
        g_chain.at[7 + quad, 0],
        quad_recv,
        bound_send_sem.at[2],
        bound_recv_sem.at[2],
        quad_device,
    )
    start(bound_copies, 1)
    pl.when(inside)(quad_copy.start)

    def set_ends(ends, into):
        for level in range(3):
            into[(0, 6, 10)[level]] = ends[0, level]
            into[(5, 9, 12)[level]] = ends[1, level]

    def near_end(tile, row, col):
        fill_tile(tile, row, col, LEAF)
        near[:, row : row + LEAF] += lax.dot_general(
            field[1, :, col : col + LEAF].astype(bf16),
            tile[:, 0:LEAF],
            NT,
            preferred_element_type=f32,
        )

    def finish_ends():
        receive(near_copies)

        @pl.when(device == 0)
        def _():
            field[:, :, 0:LEAF] = jnp.zeros((2, 8, LEAF), f32)
            edge_recv[0] = jnp.zeros((3, 2, 8, 128), f32)

        @pl.when(device == total - 1)
        def _():
            field[:, :, last + LEAF : last + 2 * LEAF] = jnp.zeros((2, 8, LEAF), f32)
            edge_recv[1] = jnp.zeros((3, 2, 8, 128), f32)

        near_end(tile_c, 0, 0)
        near_end(tile_a, last - LEAF, last + LEAF)

        receive(edge_copies)
        set_ends(edge_recv, chain)
        for at, slot in [(0, 1), (3, 4), (4, 7), (5, 8), (6, 11)]:
            local[at] = cousins(chain, slot)

    @pl.when(early == 1)
    def _():
        lax.fori_loop(ahead, 3, near_step, 0)
        set_inner()
        finish_ends()

    later = to_later[0] + to_later[1]

    @pl.when(later > 0)
    def _():
        pl.semaphore_wait(ready, 4 * later)

    for turn in range(2):

        @pl.when(to_later[turn] == 1)
        def _(turn=turn):
            far_each(turn, lambda k: far_copy(k).start())

    @pl.when(early == 0)
    def _():
        lax.fori_loop(0, 3, near_step, 0)
        set_inner()
        set_leaf_paths()
        finish_ends()

    top_column = swapped_record.T[:64]
    tx, ty, tz = top_column[:, 0:1], top_column[:, 1:2], top_column[:, 2:3]

    wait_all(far_buf.at[pl.ds(1, strides - 1)], far_recv_sem.at[1])

    @pl.when(jnp.logical_not(alone))
    def _():
        first_far.wait_recv()

    top_coef, top_skel = [], []
    for k in range(0, strides, 2):
        halves = []
        for at in (k, k + 1):
            apart = far_from[at] - box
            counts = jnp.logical_or(apart >= 2, apart <= -2)
            halves.append((far_buf[at], counts))
        (one, one_counts), (two, two_counts) = halves
        coef = jnp.where(low, jnp.where(one_counts, one, 0.0), jnp.where(two_counts, two, 0.0))
        top_coef.append(pltpu.roll(coef, 64, 1))
        top_skel.append(jnp.where(low, two, one))
    top_tile = jnp.concatenate(
        [phi(tx, ty, tz, s[0:1], s[1:2], s[2:3], far_scale) for s in top_skel], axis=1
    )
    top = mm(jnp.concatenate(top_coef, axis=1), split(top_tile), NT)
    part_buf[member] = jnp.concatenate([top, jnp.zeros((8, 64), f32)], axis=1)
    for at in range(MEMBERS - 1):
        mate = box * MEMBERS + at + jnp.where(member <= at, 1, 0)
        send(part_buf.at[member], part_buf.at[member], part_send_sem, part_recv_sem, mate)

    wait_all(u_buf.at[pl.ds(0, MEMBERS - 1)], u_send_sem)
    wait_all(g_buf.at[pl.ds(0, MEMBERS - 1)], g_send_sem)
    wait_all(far_buf.at[pl.ds(1, strides - 1)], far_send_sem.at[1])
    for copies, at in ((near_copies, 0), (edge_copies, 0), (bound_copies, 1)):
        for copy, has in zip(copies, (after[at], before[at])):
            pl.when(has)(copy.wait_send)
    pl.when(inside)(quad_copy.wait_send)

    @pl.when(jnp.logical_not(alone))
    def _():
        first_far.wait_send()

    receive(bound_copies, 1)
    pl.when(inside)(quad_copy.wait_recv)
    start_skel = jnp.where(before[1], bound_recv[0, 1], 0.0)
    end_skel = jnp.where(after[1], bound_recv[1, 1], 0.0)
    g_chain[10, 0] = jnp.where(before[1], bound_recv[0, 0], 0.0)
    g_chain[10, 1] = start_skel
    g_chain[12, 0] = jnp.where(after[1], bound_recv[1, 0], 0.0)
    g_chain[12, 1] = end_skel
    quad_coef = jnp.where(inside, quad_recv[...], 0.0)
    g_chain[6, 0] = quad_coef
    g_chain[6, 1] = pltpu.roll(start_skel, 5, 0)
    g_chain[9, 0] = quad_coef
    g_chain[9, 1] = pltpu.roll(end_skel, 5, 0)

    @pl.when(jnp.logical_not(inside))
    def _():
        for slot in (0, 5):
            g_chain[slot] = jnp.zeros((2, 8, 128), f32)

    @pl.when(open_rim)
    def _():
        for copy in rim_copies:
            copy.wait_send()
        for t in range(2):
            pltpu.make_async_remote_copy(
                src_ref=g_buf.at[member],
                dst_ref=rim_recv.at[t],
                send_sem=rim_send_sem.at[t],
                recv_sem=rim_recv_sem.at[t],
                device_id=(rim_devices[t],),
                device_id_type=MESH,
            ).wait_recv()
        even, odd = rim_recv[0], rim_recv[1]
        rim_coef = jnp.where(low, even, odd)
        rim_skel = pltpu.roll(jnp.where(low, odd, even), 64, 1)
        for slot in (0, 5):
            g_chain[slot, 0] = rim_coef
            g_chain[slot, 1] = rim_skel

    local3 = cousins(g_chain, 1 + y)
    local4 = cousins(g_chain, 7 + quad)
    local5 = cousins(g_chain, 11)
    y2 = local[6]
    y1 = [x + local[4 + at] for at, x in enumerate(lower([y2], maps[1]))]
    y0 = [x + local[at] for at, x in enumerate(lower(y1, maps[0]))]
    y4 = local4 + mm(side(local5, quad), maps[4], NT)
    y3 = local3 + mm(side(y4, rem(y, 2)), maps[3], NT)
    y3 = jnp.where(core == 1, y3, pltpu.roll(y3, 64, 1))

    wait_all(part_buf.at[pl.ds(0, MEMBERS - 1)], part_recv_sem)
    parts = [part_buf[at] for at in range(MEMBERS)]
    while len(parts) > 1:
        parts = [a + b for a, b in zip(parts[0::2], parts[1::2])]
    d6 = parts[0]
    d63 = jnp.where(low, d6, y3)
    d0 = jnp.concatenate(y0, axis=1) + mm(d63, (leaf_high, leaf_low), NN)
    for p in range(4):
        pair = d0[:, 128 * p : 128 * p + 128]
        two = jnp.concatenate([jnp.where(low, pair, 0.0), jnp.where(low, 0.0, pair)], axis=0)
        rows = lax.dot_general(
            two.astype(bf16),
            basis[128 * p : 128 * p + 128, :],
            NN,
            preferred_element_type=f32,
        )
        for t in range(2):
            leaf = 2 * p + t
            at = leaf * LEAF
            out_ref[:, at : at + LEAF] = jnp.where(
                slots < occ[leaf], near[:, at : at + LEAF] + rows[8 * t : 8 * t + 8], 0.0
            )

    wait_all(part_buf.at[pl.ds(0, MEMBERS - 1)], part_send_sem)


def body(boxes, across, coords, loads, occupancy, basis, transfer):
    strides = boxes // MEMBERS
    hbm = pl.BlockSpec(memory_space=pl.ANY)
    dma = pltpu.SemaphoreType.DMA
    return pl.pallas_call(
        functools.partial(kernel, boxes, across),
        out_shape=jax.ShapeDtypeStruct((COLS, OWN), f32),
        in_specs=[hbm] * 5,
        out_specs=pl.BlockSpec(memory_space=pltpu.VMEM),
        scratch_shapes=[
            pltpu.VMEM((3, OWN), f32),
            pltpu.VMEM((COLS, OWN), bf16),
            pltpu.SMEM((LEAVES,), jnp.int32),
            pltpu.VMEM((LEAVES * 64, LEAF), bf16),
            pltpu.VMEM((6, 128, 64), f32),
            pltpu.VMEM((6, 128, 128), bf16),
            pltpu.VMEM((6, 128, 128), bf16),
            pltpu.VMEM((128, 128), f32),
            pltpu.VMEM((2, 8, OWN + 2 * LEAF), f32),
            pltpu.VMEM((OWN, 8), f32),
            pltpu.VMEM((128, 512), bf16),
            pltpu.VMEM((128, 512), bf16),
            pltpu.VMEM((COLS, OWN + LEAF), f32),
            pltpu.VMEM((LEAF, 2 * LEAF), bf16),
            pltpu.VMEM((LEAF, 2 * LEAF), bf16),
            pltpu.VMEM((LEAF, LEAF), bf16),
            pltpu.VMEM((13, 2, 8, 128), f32),
            pltpu.VMEM((13, 2, 8, 128), f32),
            pltpu.VMEM((7, 8, 128), f32),
            pltpu.VMEM((2, 3, 2, 8, 128), f32),
            pltpu.VMEM((2, 3, 2, 8, 128), f32),
            pltpu.VMEM((MEMBERS, 8, 128), f32),
            pltpu.VMEM((MEMBERS, 8, 128), f32),
            pltpu.VMEM((2, 2, 8, 128), f32),
            pltpu.VMEM((2, 2, 8, 128), f32),
            pltpu.VMEM((8, 128), f32),
            pltpu.VMEM((2, 8, 128), f32),
            pltpu.VMEM((2, 8, 128), f32),
            pltpu.VMEM((strides, 8, 128), f32),
            pltpu.VMEM((MEMBERS, 8, 128), f32),
            dma((5,)),
            dma((2,)),
            dma((2,)),
            dma((2,)),
            dma((2,)),
            dma,
            dma,
            dma,
            dma,
            dma((3,)),
            dma((3,)),
            dma((2,)),
            dma((2,)),
            dma((2,)),
            dma((2,)),
            dma,
            dma,
            pltpu.SemaphoreType.REGULAR,
        ],
        compiler_params=pltpu.CompilerParams(
            collective_id=0, has_side_effects=True, vmem_limit_bytes=32 * 1024 * 1024
        ),
    )(
        *[
            pltpu.with_memory_space_constraint(x, pltpu.HBM)
            for x in (
                coords,
                loads,
                occupancy,
                basis.reshape(LEAVES * 64, LEAF),
                transfer.reshape(6, 128, 64),
            )
        ]
    )


def solution(mesh):
    boxes = mesh.shape["box"] // MEMBERS
    return jax.shard_map(
        functools.partial(body, boxes, 4),
        mesh=mesh,
        in_specs=(P(None, "box"), P(None, "box"), P("box"), P("box", None, None), P()),
        out_specs=P(None, "box"),
        check_vma=False,
    )
```

profile of v0, /device:TPU:1, one launch (start us, length us, event | category | flops | bytes accessed | tf_op | source)
XLA Modules:
  0.0 28.9 jit_solution(1985715513634644681)
XLA Ops:
  0.0 28.3 %shard_map.55 = f32[8,2048]{1,0:T(8,128)S(1)} custom-call(f32[3,2048]{1,0:T(4,128)} %coords_hbm.1, bf16[8,2048]{1,0:T(8,128)(2,1)} %loads_hbm.1, s32[8]{0:T(128)} %occ_hbm.1, bf16[512,256]{1,0:T(8,128)(2,1)} %bitcast.3, f32[6,128,64]{2,1,0:T(8,128)} %bitcast.2), custom_call_target="tpu_custom_call" | custom-call | tf_op jit(solution)/shard_map/pallas_call | solution.py:770
  28.3 0.6 %copy.7 = f32[8,2048]{1,0:T(8,128)} copy(f32[8,2048]{1,0:T(8,128)S(1)} %shard_map.55) | data formatting | bytes 131072
where the time goes:
time: 29 us; the launch traced here: 28.9 us
  Pallas kernels  28.3 us (98%)
  local copies, waits for them, and re-layouts  0.63 us (2%)
    pallas_call x1, Pallas kernels, body(): pl.pallas_call(functools.partial(kernel, boxes, across), out_shape=jax.Sh...  28.3 us
    unnamed x1, local copies, waits for them, and re-layouts  0.63 us

commit v1 on v0

--- a/solution.py
+++ b/solution.py
@@ -207,7 +207,7 @@
 
     def far_depths(side):
         first = 4 * rem(side + z_high, 2) + 2 * core
-        return [first + z_low, first + 1 - z_low]
+        return [first, first + 1]
 
     to_z, from_z = far_depths(side_to), far_depths(side_from)
 
@@ -233,10 +233,12 @@
 
     def far_each(turn, act):
         for k in far_order[4 * turn : 4 * turn + 4]:
-            if k:
+            if k == turn:
+                pl.when(jnp.logical_not(jnp.logical_and(alone, z_low == turn)))(
+                    functools.partial(act, k)
+                )
+            else:
                 act(k)
-            else:
-                pl.when(jnp.logical_not(alone))(functools.partial(act, 0))
 
     for turn in range(2):
 
@@ -327,6 +329,12 @@
     u_buf[member] = mm(c2[0], split(map_6), NN) + s6
     path_map[...] = map_6
 
+    set_map(2)
+    every_eighth = (index == (lanes & 63) * 8).astype(f32).astype(bf16)
+    s3 = pick(jnp.concatenate(s0, axis=1), every_eighth)
+    c3 = raise_coef(c2, maps[2])[0]
+    g_buf[member] = jnp.where(half == core, c3, s3)
+
     def set_field():
         field[0, :, LEAF : LEAF + OWN] = points
         for leaf in range(LEAVES):
@@ -445,14 +453,12 @@
     def wait_all(ref, semaphore):
         pltpu.make_async_copy(ref, ref, semaphore).wait()
 
-    for mate in mates:
+    first = (6, 2, 7, 3, 0, 4, 1, 5)
+    place = sum(jnp.where(member == at, rank, 0) for rank, at in enumerate(first))
+    for rank in range(MEMBERS - 1):
+        mate = box * MEMBERS + jnp.where(place <= rank, first[rank + 1], first[rank])
         send(u_buf.at[member], u_buf.at[member], u_send_sem, u_recv_sem, mate)
 
-    set_map(2)
-    every_eighth = (index == (lanes & 63) * 8).astype(f32).astype(bf16)
-    s3 = pick(jnp.concatenate(s0, axis=1), every_eighth)
-    c3 = raise_coef(c2, maps[2])[0]
-    g_buf[member] = jnp.where(half == core, c3, s3)
     for mate in mates:
         send(g_buf.at[member], g_buf.at[member], g_send_sem, g_recv_sem, mate)
 
@@ -532,23 +538,25 @@
         parts = [a + b for a, b in zip(parts[0::2], parts[1::2])]
     top_record = parts[0]
     swapped_record = pltpu.roll(top_record, 64, 1)
-    far_send[0] = top_record
-    far_send[1] = swapped_record
+    far_send[...] = jnp.where(z_low == 0, top_record, swapped_record)
 
     @pl.when(alone)
     def _():
-        far_buf[0] = far_send[0]
+        far_buf[z_low] = far_send[...]
 
     def far_copy(k):
-        return remote(
-            far_send.at[k % 2],
-            far_buf.at[k],
-            far_send_sem.at[min(k, 1)],
-            far_recv_sem.at[min(k, 1)],
-            far_to[k],
-        )
-
-    first_far = far_copy(0)
+        slot = k - k % 2 + z_low
+        return remote(far_send, far_buf.at[slot], far_send_sem, far_recv_sem, far_to[k])
+
+    def far_wait(semaphore):
+        @pl.when(alone)
+        def _():
+            wait_all(far_buf.at[pl.ds(1, strides - 1)], semaphore)
+
+        @pl.when(jnp.logical_not(alone))
+        def _():
+            wait_all(far_buf, semaphore)
+
     for turn in range(2):
 
         @pl.when(to_later[turn] == 0)
@@ -650,11 +658,7 @@
     top_column = swapped_record.T[:64]
     tx, ty, tz = top_column[:, 0:1], top_column[:, 1:2], top_column[:, 2:3]
 
-    wait_all(far_buf.at[pl.ds(1, strides - 1)], far_recv_sem.at[1])
-
-    @pl.when(jnp.logical_not(alone))
-    def _():
-        first_far.wait_recv()
+    far_wait(far_recv_sem)
 
     top_coef, top_skel = [], []
     for k in range(0, strides, 2):
@@ -678,15 +682,11 @@
 
     wait_all(u_buf.at[pl.ds(0, MEMBERS - 1)], u_send_sem)
     wait_all(g_buf.at[pl.ds(0, MEMBERS - 1)], g_send_sem)
-    wait_all(far_buf.at[pl.ds(1, strides - 1)], far_send_sem.at[1])
+    far_wait(far_send_sem)
     for copies, at in ((near_copies, 0), (edge_copies, 0), (bound_copies, 1)):
         for copy, has in zip(copies, (after[at], before[at])):
             pl.when(has)(copy.wait_send)
     pl.when(inside)(quad_copy.wait_send)
-
-    @pl.when(jnp.logical_not(alone))
-    def _():
-        first_far.wait_send()
 
     receive(bound_copies, 1)
     pl.when(inside)(quad_copy.wait_recv)
@@ -800,7 +800,7 @@
             pltpu.VMEM((2, 2, 8, 128), f32),
             pltpu.VMEM((8, 128), f32),
             pltpu.VMEM((2, 8, 128), f32),
-            pltpu.VMEM((2, 8, 128), f32),
+            pltpu.VMEM((8, 128), f32),
             pltpu.VMEM((strides, 8, 128), f32),
             pltpu.VMEM((MEMBERS, 8, 128), f32),
             dma((5,)),
@@ -816,8 +816,8 @@
             dma((3,)),
             dma((2,)),
             dma((2,)),
-            dma((2,)),
-            dma((2,)),
+            dma,
+            dma,
             dma,
             dma,
             pltpu.SemaphoreType.REGULAR,

time: 29 us -> 28.8 us (level); the launches traced: 28.9 us -> 28.4 us
  Pallas kernels: 28.3 us -> 27.7 us
    pallas_call x1, Pallas kernels: 28.3 us -> 27.7 us  [body(): pl.pallas_call(functools.partial(kernel, boxes, across), out_shape=jax.Sh...]
where the time goes in v1:
time: 28.8 us; the launch traced here: 28.4 us
  Pallas kernels  27.7 us (96%)
  local copies, waits for them, and re-layouts  0.63 us (2%)
    pallas_call x1, Pallas kernels, body(): pl.pallas_call(functools.partial(kernel, boxes, across), out_shape=jax.Sh...  27.7 us
    unnamed x1, local copies, waits for them, and re-layouts  0.63 us

profile of v1, /device:TPU:1, one launch (start us, length us, event | category | flops | bytes accessed | tf_op | source)
XLA Modules:
  0.0 28.4 jit_solution(15937488734175034829)
XLA Ops:
  0.0 27.7 %shard_map.55 = f32[8,2048]{1,0:T(8,128)S(1)} custom-call(f32[3,2048]{1,0:T(4,128)} %coords_hbm.1, bf16[8,2048]{1,0:T(8,128)(2,1)} %loads_hbm.1, s32[8]{0:T(128)} %occ_hbm.1, bf16[512,256]{1,0:T(8,128)(2,1)} %bitcast.3, f32[6,128,64]{2,1,0:T(8,128)} %bitcast.2), custom_call_target="tpu_custom_call" | custom-call | tf_op jit(solution)/shard_map/pallas_call | solution.py:770
  27.7 0.6 %copy.7 = f32[8,2048]{1,0:T(8,128)} copy(f32[8,2048]{1,0:T(8,128)S(1)} %shard_map.55) | data formatting | bytes 131072

commit v2 on v1

--- a/solution.py
+++ b/solution.py
@@ -261,7 +261,7 @@
     rim_devices = [rim_box * MEMBERS + 6 - 6 * top + t for t in range(2)]
     quad = div(member, 4)
     quad_device = rem(box + boxes + 2 * quad - 1, boxes) * MEMBERS + mirror
-    early = jnp.where(z == 0, 1, 0)
+    early = jnp.where(z <= 1, 1, 0)
     ahead = 2
     before = [device > 0, box > 0]
     after = [device < total - 1, box < boxes - 1]

time: 28.8 us -> 28.8 us (level)
  no operation moved by 1% of the time
where the time goes in v2:
time: 28.8 us; the launch traced here: 28.5 us
  Pallas kernels  27.9 us (97%)
  local copies, waits for them, and re-layouts  0.63 us (2%)
    pallas_call x1, Pallas kernels, body(): pl.pallas_call(functools.partial(kernel, boxes, across), out_shape=jax.Sh...  27.9 us
    unnamed x1, local copies, waits for them, and re-layouts  0.63 us

profile of v2, /device:TPU:1, one launch (start us, length us, event | category | flops | bytes accessed | tf_op | source)
XLA Modules:
  0.0 28.5 jit_solution(5129932141664079285)
XLA Ops:
  0.0 27.9 %shard_map.55 = f32[8,2048]{1,0:T(8,128)S(1)} custom-call(f32[3,2048]{1,0:T(4,128)} %coords_hbm.1, bf16[8,2048]{1,0:T(8,128)(2,1)} %loads_hbm.1, s32[8]{0:T(128)} %occ_hbm.1, bf16[512,256]{1,0:T(8,128)(2,1)} %bitcast.3, f32[6,128,64]{2,1,0:T(8,128)} %bitcast.2), custom_call_target="tpu_custom_call" | custom-call | tf_op jit(solution)/shard_map/pallas_call | solution.py:770
  27.9 0.6 %copy.7 = f32[8,2048]{1,0:T(8,128)} copy(f32[8,2048]{1,0:T(8,128)S(1)} %shard_map.55) | data formatting | bytes 131072

commit v3 on v1

--- a/solution.py
+++ b/solution.py
@@ -544,9 +544,22 @@
     def _():
         far_buf[z_low] = far_send[...]
 
-    def far_copy(k):
-        slot = k - k % 2 + z_low
-        return remote(far_send, far_buf.at[slot], far_send_sem, far_recv_sem, far_to[k])
+    def far_start(later):
+        for to_x in (0, 3, 1, 2):
+            slot = 2 * rem(to_x + across - x, across) + z_low
+            for turn in range(2):
+                own = jnp.logical_and(alone, jnp.logical_and(x == to_x, z_low == turn))
+
+                @pl.when(jnp.logical_and(to_later[turn] == later, jnp.logical_not(own)))
+                def _(to_x=to_x, turn=turn, slot=slot):
+                    there = (to_x * depth + to_z[turn]) * 2 + far_half
+                    remote(
+                        far_send,
+                        far_buf.at[slot],
+                        far_send_sem,
+                        far_recv_sem,
+                        there * MEMBERS + far_member,
+                    ).start()
 
     def far_wait(semaphore):
         @pl.when(alone)
@@ -557,11 +570,7 @@
         def _():
             wait_all(far_buf, semaphore)
 
-    for turn in range(2):
-
-        @pl.when(to_later[turn] == 0)
-        def _(turn=turn):
-            far_each(turn, lambda k: far_copy(k).start())
+    far_start(0)
 
     wait_all(g_buf.at[pl.ds(0, MEMBERS - 1)], g_recv_sem)
     c3s, s3s = [], []
@@ -642,11 +651,7 @@
     def _():
         pl.semaphore_wait(ready, 4 * later)
 
-    for turn in range(2):
-
-        @pl.when(to_later[turn] == 1)
-        def _(turn=turn):
-            far_each(turn, lambda k: far_copy(k).start())
+    far_start(1)
 
     @pl.when(early == 0)
     def _():

time: 28.8 us -> 28.8 us (level)
  no operation moved by 1% of the time
where the time goes in v3:
time: 28.8 us; the launch traced here: 28.5 us
  Pallas kernels  27.9 us (97%)
  local copies, waits for them, and re-layouts  0.63 us (2%)
    pallas_call x1, Pallas kernels, body(): pl.pallas_call(functools.partial(kernel, boxes, across), out_shape=jax.Sh...  27.9 us
    unnamed x1, local copies, waits for them, and re-layouts  0.63 us

profile of v3, /device:TPU:1, one launch (start us, length us, event | category | flops | bytes accessed | tf_op | source)
XLA Modules:
  0.0 28.5 jit_solution(8681852764746956108)
XLA Ops:
  0.0 27.9 %shard_map.55 = f32[8,2048]{1,0:T(8,128)S(1)} custom-call(f32[3,2048]{1,0:T(4,128)} %coords_hbm.1, bf16[8,2048]{1,0:T(8,128)(2,1)} %loads_hbm.1, s32[8]{0:T(128)} %occ_hbm.1, bf16[512,256]{1,0:T(8,128)(2,1)} %bitcast.3, f32[6,128,64]{2,1,0:T(8,128)} %bitcast.2), custom_call_target="tpu_custom_call" | custom-call | tf_op jit(solution)/shard_map/pallas_call | solution.py:775
  27.9 0.6 %copy.7 = f32[8,2048]{1,0:T(8,128)} copy(f32[8,2048]{1,0:T(8,128)S(1)} %shard_map.55) | data formatting | bytes 131072

commit v4 on v1

--- a/solution.py
+++ b/solution.py
@@ -329,12 +329,6 @@
     u_buf[member] = mm(c2[0], split(map_6), NN) + s6
     path_map[...] = map_6
 
-    set_map(2)
-    every_eighth = (index == (lanes & 63) * 8).astype(f32).astype(bf16)
-    s3 = pick(jnp.concatenate(s0, axis=1), every_eighth)
-    c3 = raise_coef(c2, maps[2])[0]
-    g_buf[member] = jnp.where(half == core, c3, s3)
-
     def set_field():
         field[0, :, LEAF : LEAF + OWN] = points
         for leaf in range(LEAVES):
@@ -459,6 +453,11 @@
         mate = box * MEMBERS + jnp.where(place <= rank, first[rank + 1], first[rank])
         send(u_buf.at[member], u_buf.at[member], u_send_sem, u_recv_sem, mate)
 
+    set_map(2)
+    every_eighth = (index == (lanes & 63) * 8).astype(f32).astype(bf16)
+    s3 = pick(jnp.concatenate(s0, axis=1), every_eighth)
+    c3 = raise_coef(c2, maps[2])[0]
+    g_buf[member] = jnp.where(half == core, c3, s3)
     for mate in mates:
         send(g_buf.at[member], g_buf.at[member], g_send_sem, g_recv_sem, mate)
 

time: 28.8 us -> 28.8 us (level)
  Pallas kernels: 27.7 us -> 28 us
where the time goes in v4:
time: 28.8 us; the launch traced here: 28.6 us
  Pallas kernels  28 us (97%)
  local copies, waits for them, and re-layouts  0.63 us (2%)
    pallas_call x1, Pallas kernels, body(): pl.pallas_call(functools.partial(kernel, boxes, across), out_shape=jax.Sh...  28 us
    unnamed x1, local copies, waits for them, and re-layouts  0.63 us

profile of v4, /device:TPU:1, one launch (start us, length us, event | category | flops | bytes accessed | tf_op | source)
XLA Modules:
  0.0 28.6 jit_solution(10131609645825616027)
XLA Ops:
  0.0 28.0 %shard_map.55 = f32[8,2048]{1,0:T(8,128)S(1)} custom-call(f32[3,2048]{1,0:T(4,128)} %coords_hbm.1, bf16[8,2048]{1,0:T(8,128)(2,1)} %loads_hbm.1, s32[8]{0:T(128)} %occ_hbm.1, bf16[512,256]{1,0:T(8,128)(2,1)} %bitcast.3, f32[6,128,64]{2,1,0:T(8,128)} %bitcast.2), custom_call_target="tpu_custom_call" | custom-call | tf_op jit(solution)/shard_map/pallas_call | solution.py:769
  28.0 0.6 %copy.7 = f32[8,2048]{1,0:T(8,128)} copy(f32[8,2048]{1,0:T(8,128)S(1)} %shard_map.55) | data formatting | bytes 131072

commit v5 on v4

--- a/solution.py
+++ b/solution.py
@@ -333,6 +333,8 @@
         field[0, :, LEAF : LEAF + OWN] = points
         for leaf in range(LEAVES):
             field[1, :, (leaf + 1) * LEAF : (leaf + 2) * LEAF] = live[leaf]
+
+    def set_column():
         for at in range(0, OWN, 128):
             column[at : at + 128, :] = points[:, at : at + 128].T
         near[...] = jnp.zeros_like(near)
@@ -408,6 +410,7 @@
     @pl.when(early == 1)
     def _():
         set_field()
+        set_column()
         lax.fori_loop(0, ahead, near_step, 0)
 
     pl.semaphore_wait(
@@ -524,9 +527,6 @@
     set_edges()
     start(edge_copies)
 
-    set_map(3)
-    set_map(4)
-
     @pl.when(early == 1)
     def _():
         set_leaf_paths()
@@ -562,6 +562,8 @@
         def _(turn=turn):
             far_each(turn, lambda k: far_copy(k).start())
 
+    set_map(3)
+    set_map(4)
     wait_all(g_buf.at[pl.ds(0, MEMBERS - 1)], g_recv_sem)
     c3s, s3s = [], []
     for p in range(4):
@@ -649,6 +651,7 @@
 
     @pl.when(early == 0)
     def _():
+        set_column()
         lax.fori_loop(0, 3, near_step, 0)
         set_inner()
         set_leaf_paths()

time: 28.8 us -> 29 us (level)
  no operation moved by 1% of the time
where the time goes in v5:
time: 29 us; the launch traced here: 28.6 us
  Pallas kernels  28 us (97%)
  local copies, waits for them, and re-layouts  0.63 us (2%)
    pallas_call x1, Pallas kernels, body(): pl.pallas_call(functools.partial(kernel, boxes, across), out_shape=jax.Sh...  28 us
    unnamed x1, local copies, waits for them, and re-layouts  0.63 us

profile of v5, /device:TPU:1, one launch (start us, length us, event | category | flops | bytes accessed | tf_op | source)
XLA Modules:
  0.0 28.6 jit_solution(12037469938389707472)
XLA Ops:
  0.0 28.0 %shard_map.55 = f32[8,2048]{1,0:T(8,128)S(1)} custom-call(f32[3,2048]{1,0:T(4,128)} %coords_hbm.1, bf16[8,2048]{1,0:T(8,128)(2,1)} %loads_hbm.1, s32[8]{0:T(128)} %occ_hbm.1, bf16[512,256]{1,0:T(8,128)(2,1)} %bitcast.3, f32[6,128,64]{2,1,0:T(8,128)} %bitcast.2), custom_call_target="tpu_custom_call" | custom-call | tf_op jit(solution)/shard_map/pallas_call | solution.py:772
  28.0 0.6 %copy.7 = f32[8,2048]{1,0:T(8,128)} copy(f32[8,2048]{1,0:T(8,128)S(1)} %shard_map.55) | data formatting | bytes 131072

commit v6 on v4

--- a/solution.py
+++ b/solution.py
@@ -173,11 +173,11 @@
         pltpu.make_async_copy(src, dst, load_sem.at[at])
         for at, (src, dst) in enumerate(
             [
-                (coords_hbm, coords),
-                (transfer_hbm, transfer),
                 (loads_hbm, loads),
                 (occ_hbm, occ),
                 (basis_hbm, basis),
+                (coords_hbm, coords),
+                (transfer_hbm, transfer),
             ]
         )
     ]
@@ -286,25 +286,14 @@
     every_second = (
         (lax.broadcasted_iota(jnp.int32, (128, 128), 0) == picks).astype(f32).astype(bf16)
     )
-    for copy in loading:
-        copy.wait()
-    points = jnp.concatenate([coords[...], jnp.zeros((5, OWN), f32)], axis=0)
-    s0 = [
-        jnp.concatenate(
-            [points[:, 512 * p : 512 * p + 64], points[:, 512 * p + 256 : 512 * p + 320]], axis=1
-        )
-        for p in range(4)
-    ]
-    s6 = pick(jnp.concatenate(s0, axis=1), placed)
-
     maps = [(map_high.at[level], map_low.at[level]) for level in range(6)]
 
     def set_map(level):
         once = transfer[level]
         map_high[level], map_low[level] = split(jnp.concatenate([once, once], axis=1))
 
-    for level in range(2):
-        set_map(level)
+    for copy in loading[:3]:
+        copy.wait()
     slots = lax.broadcasted_iota(jnp.int32, (COLS, LEAF), 1)
     live = []
     for leaf in range(LEAVES):
@@ -317,6 +306,19 @@
             two, basis[128 * p : 128 * p + 128, :], NT, preferred_element_type=f32
         )
         c0.append(jnp.where(low, rows[:8], rows[8:]))
+    for copy in loading[3:]:
+        copy.wait()
+    points = jnp.concatenate([coords[...], jnp.zeros((5, OWN), f32)], axis=0)
+    s0 = [
+        jnp.concatenate(
+            [points[:, 512 * p : 512 * p + 64], points[:, 512 * p + 256 : 512 * p + 320]], axis=1
+        )
+        for p in range(4)
+    ]
+    s6 = pick(jnp.concatenate(s0, axis=1), placed)
+
+    for level in range(2):
+        set_map(level)
     c1 = raise_coef(c0, maps[0])
     c2 = raise_coef(c1, maps[1])
     def factor(level, at):

time: 28.8 us -> 28.8 us (level)
  no operation moved by 1% of the time
where the time goes in v6:
time: 28.8 us; the launch traced here: 28.6 us
  Pallas kernels  28 us (97%)
  local copies, waits for them, and re-layouts  0.63 us (2%)
    pallas_call x1, Pallas kernels, body(): pl.pallas_call(functools.partial(kernel, boxes, across), out_shape=jax.Sh...  28 us
    unnamed x1, local copies, waits for them, and re-layouts  0.63 us

profile of v6, /device:TPU:1, one launch (start us, length us, event | category | flops | bytes accessed | tf_op | source)
XLA Modules:
  0.0 28.6 jit_solution(8911953553193087216)
XLA Ops:
  0.0 28.0 %shard_map.55 = f32[8,2048]{1,0:T(8,128)S(1)} custom-call(f32[3,2048]{1,0:T(4,128)} %coords_hbm.1, bf16[8,2048]{1,0:T(8,128)(2,1)} %loads_hbm.1, s32[8]{0:T(128)} %occ_hbm.1, bf16[512,256]{1,0:T(8,128)(2,1)} %bitcast.3, f32[6,128,64]{2,1,0:T(8,128)} %bitcast.2), custom_call_target="tpu_custom_call" | custom-call | tf_op jit(solution)/shard_map/pallas_call | solution.py:771
  28.0 0.6 %copy.7 = f32[8,2048]{1,0:T(8,128)} copy(f32[8,2048]{1,0:T(8,128)S(1)} %shard_map.55) | data formatting | bytes 131072
